TPU v7x, 32 devices: a whole 2x2x4 slice. The times are simulated.
32 devices in a mesh: film: 2 (over y), site: 4 (over z), pair: 2 (over x), orb: 2 (over core).
Axes of the slice: x: 2, y: 2, z: 4, core: 2. Of those that a mesh axis runs over, the one named last changes fastest.
Arguments:
- coeff: bfloat16 [512, 16, 256], P(('film', 'site'), 'orb'), parts along dimension 0, may hold values from -0.375 to 0.375
- fock_pair: bfloat16 [512, 2, 256, 256], P(('film', 'site'), 'pair'), parts along dimension 0, may hold values from -6 to 6
- fock_site: bfloat16 [512, 256, 256], P(('film', 'site', 'pair')), parts along dimension 0, may hold values from -6 to 6
- pair_right: int32 [512, 2], P(('film', 'site'), 'pair'), parts along dimension 0, may hold values from -1 to 255, as said below
Outputs:
- coupling: float32 [512, 16, 4, 16], P(('film', 'site'), None, 'pair', 'orb'), parts along dimension 0
- site_energy: float32 [512, 16], P(('film', 'site', 'pair'), 'orb'), parts along dimension 0
There are 2 independent parts, one for each index of `film`. A program takes and returns all parts, laid end to end along the dimension named above; each array names one. Nothing has to cross between parts.
Inputs may be any that keep to these rules, and one draw needn't show every extreme that they name: pair_right[m, q] is -1 (no pair in entry q) or the molecule paired with m there, never m itself; within one column q every molecule is named at most once; within one column, the 64 molecules of one site group name at most 16 molecules of any one site group.
All inputs are finite; a program needn't handle non-finite values.
Results may differ from a plain program's by a relative error of at most 0.0003.
Values may be sent and summed in bfloat16 or wider, within the bound.
A program may use at most 64 MiB of HBM per device.

v0:
```python
import jax
import jax.numpy as jnp
from jax import lax
from jax.sharding import PartitionSpec as P


def swapped(value, axis, apart):
    mask = 2**apart
    pairs = [(source, source ^ mask) for source in range(lax.axis_size(axis))]
    return lax.ppermute(value, axis, pairs)


def trade_halves(full_rows):
    width = full_rows.shape[2]
    orb_index = lax.axis_index("orb")
    keep_part = lax.dynamic_slice_in_dim(full_rows, orb_index * width, width, 1)
    send_part = lax.dynamic_slice_in_dim(full_rows, (1 - orb_index) * width, width, 1)
    partner_part = swapped(send_part, "orb", 0)
    first = jnp.concatenate([keep_part, partner_part], axis=2)
    second = jnp.concatenate([partner_part, keep_part], axis=2)
    return jnp.where(orb_index == 0, first, second)


def left_products(
    right_panels, whole_orbs, blocks, columns, target_site, bucket_slot, site_count, bucket
):
    orb_count = whole_orbs.shape[1]
    half_orbs = right_panels.shape[1]
    image = jnp.einsum("euv,ebv->eub", blocks, right_panels, preferred_element_type=jnp.float32)
    left_wide = jnp.repeat(whole_orbs.astype(jnp.float32), columns, axis=0)
    row_left = jnp.einsum("eau,eub->eab", left_wide, image, precision=lax.Precision.HIGHEST)
    own_rows = trade_halves(row_left)
    payload = jnp.swapaxes(own_rows, 1, 2)
    outgoing = (
        jnp.zeros((site_count, bucket, orb_count, half_orbs), jnp.float32)
        .at[target_site, bucket_slot]
        .set(payload, mode="drop")
    )
    return (row_left, outgoing)


def local(coeff, fock_pair, fock_site, pair_right):
    group_size, half_orbs, basis_len = coeff.shape
    columns = pair_right.shape[1]
    site_count = lax.axis_size("site")
    bucket = columns * group_size // site_count
    entry_count = group_size * columns
    whole_orbs = lax.all_gather(coeff, "orb", axis=1, tiled=True)
    orb_count = whole_orbs.shape[1]
    partner = pair_right.reshape(-1)
    is_live = partner >= 0
    target_site = jnp.where(is_live, partner // group_size, site_count)
    onehot = (target_site[:, None] == jnp.arange(site_count)[None, :]).astype(jnp.int32)
    earlier = jnp.cumsum(onehot, axis=0) - onehot
    bucket_slot = jnp.sum(earlier * onehot, axis=1)
    column_of = jnp.tile(jnp.arange(columns), group_size)
    labels = jnp.where(is_live, partner % group_size * columns + column_of, -1)
    label_buffer = (
        jnp.full((site_count, bucket), -1, jnp.int32)
        .at[target_site, bucket_slot]
        .set(labels, mode="drop")
    )
    blocks = fock_pair.reshape(entry_count, basis_len, basis_len)
    gathered = lax.all_gather(coeff, "site", axis=0, tiled=True)
    right_panels = gathered[jnp.maximum(partner, 0)]
    row_left, outgoing = left_products(
        right_panels, whole_orbs, blocks, columns, target_site, bucket_slot, site_count, bucket
    )
    arrived, arrived_labels = (
        lax.all_to_all(outgoing, "site", split_axis=0, concat_axis=0, tiled=True),
        lax.all_to_all(label_buffer, "site", split_axis=0, concat_axis=0, tiled=True),
    )
    row_left = jnp.where(is_live[:, None, None], row_left, jnp.zeros_like(row_left))
    flat_labels = arrived_labels.reshape(-1)
    usable = flat_labels >= 0
    molecule_at = jnp.where(usable, flat_labels // columns, group_size)
    column_at = jnp.where(usable, flat_labels % columns, 0)
    odd_slots = (
        jnp.zeros((group_size, columns, orb_count, half_orbs), jnp.float32)
        .at[molecule_at, column_at]
        .set(arrived.reshape(-1, orb_count, half_orbs), mode="drop")
    )
    even_slots = row_left.reshape(group_size, columns, orb_count, half_orbs)
    joined = jnp.stack([even_slots, odd_slots], axis=2).reshape(
        group_size, 2 * columns, orb_count, half_orbs
    )
    coupling = jnp.transpose(joined, (0, 2, 1, 3))
    own_count = fock_site.shape[0]
    own_panels = lax.dynamic_slice_in_dim(coeff, lax.axis_index("pair") * own_count, own_count, 0)
    spread = jnp.einsum("kau,kuv->kav", own_panels, fock_site, preferred_element_type=jnp.float32)
    site_energy = jnp.sum(spread * own_panels.astype(jnp.float32), axis=2)
    return (coupling, site_energy)


def solution(mesh):
    return jax.shard_map(
        local,
        mesh=mesh,
        in_specs=(
            P(("film", "site"), "orb", None),
            P(("film", "site"), "pair", None, None),
            P(("film", "site", "pair"), None, None),
            P(("film", "site"), "pair"),
        ),
        out_specs=(P(("film", "site"), None, "pair", "orb"), P(("film", "site", "pair"), "orb")),
        check_vma=False,
    )
```

profile of v0, /device:TPU:0, one launch (start us, length us, event | category | flops | bytes accessed | tf_op | source)
XLA Modules:
  0.0 74.7 jit_solution(15182343379682794122)
XLA Ops:
  7.2 0.0 all-gather.2.cloned.1.call-start
  7.2 0.7 all-gather.2.cloned.1.call-update
  7.9 0.7 maximum_bitcast_fusion.1
  8.6 0.1 fusion.5
  8.6 0.1 reduce_window_sum.11
  8.7 0.2 select_reduce_fusion
  8.9 0.7 fusion.7
  9.6 0.6 broadcast_in_dim.42
  10.2 10.1 %scatter_fusion = s32[4,16]{1,0:T(4,128)} fusion(s32[4,16]{1,0:T(4,128)} %broadcast_in_dim.42, s32[64]{0:T(128)S(1)} %fusion.11, s32[64]{0:T(128)S(1)} %fusion.7), kind=kCustom, calls=%fused_computation.1 | custom fusion | bytes 1280 | tf_op jit(solution)/shard_map/scatter | solution.py:61
  20.3 6.3 %all-to-all-start = ((s32[4,1,16]{2,1,0:T(1,128)}), s32[4,1,16]{2,1,0:T(1,128)S(1)}, u32[]{:S(2)}, u32[]{:S(2)}) async-start(s32[4,1,16]{2,1,0:T(1,128)} %bitcast.9), calls=%async_computation | async-start | bytes 4096 | tf_op jit(solution)/shard_map/all_to_all | solution.py:71
  26.6 2.4 %all_gather.7 = bf16[64,16,256]{2,1,0:T(8,128)(2,1)S(1)} all-gather(bf16[64,8,256]{2,1,0:T(8,128)(2,1)} %param.4), channel_id=1, replica_groups=mesh['film'=2,'site'=4,'pair'=2,'orb'=2] {'orb'}, dimensions={1}, use_global_device_ids=true | all-gather | bytes 786432 | tf_op jit(solution)/shard_map/all_gather | solution.py:48
  29.0 0.7 bitcast_compare_fusion
  29.7 3.0 %fusion.2 = f32[32,8]{1,0:T(8,128)S(1)} fusion(bf16[32,256,256]{2,1,0:T(8,128)(2,1)} %param.6, bf16[64,8,256]{2,1,0:T(8,128)(2,1)} %param.4, s32[]{:T(128)S(6)} %select_n.112), kind=kOutput, calls=%fused_computation.7 | convolution fusion | flops 33750784 | bytes 4458496 | tf_op jit(solution)/shard_map/kau,kuv->kav/dot_general | solution.py:90
  32.6 0.7 copy.17
  33.3 0.0 all-to-all-done
  33.3 0.5 broadcast.200
  33.8 0.7 reduce.3
  34.5 0.1 reshape.75
  34.6 5.7 %all-gather.2.cloned.1.call-done = bf16[256,8,256]{2,1,0:T(8,128)(2,1)} async-done(((bf16[64,8,256]{2,1,0:T(8,128)(2,1)}), bf16[256,8,256]{2,1,0:T(8,128)(2,1)}) %all-gather.2.cloned.1.call-update) | async-done | bytes 1048592 | tf_op jit(solution)/shard_map/all_gather | solution.py:64
  40.3 1.8 %gather_fusion = bf16[64,8,256]{2,1,0:T(8,128)(2,1)S(1)} fusion(bf16[256,8,256]{2,1,0:T(8,128)(2,1)} %all-gather.2.cloned.1.call-done, s32[1024]{0:T(1024)S(1)} %pad_clamp_fusion), kind=kCustom, calls=%fused_computation | custom fusion | bytes 524544 | tf_op jit(solution)/shard_map/gather | solution.py:65
  42.1 5.6 %fusion = f32[64,8,256]{2,1,0:T(8,128)S(1)} fusion(bf16[64,8,256]{2,1,0:T(8,128)(2,1)S(1)} %gather_fusion, bf16[64,1,256,256]{3,2,1,0:T(8,128)(2,1)} %param.5), kind=kOutput, calls=%fused_computation.4 | convolution fusion | flops 67108864 | bytes 9175040 | tf_op jit(solution)/shard_map/euv,ebv->eub/dot_general | solution.py:29
  47.7 0.5 fusion.12
  48.3 0.2 dynamic-slice_bitcast_fusion.1
  48.5 0.1 collective-permute-start
  48.6 0.1 copy.9
  48.7 1.4 %collective-permute-done = f32[64,8,8]{1,2,0:T(8,128)S(1)} collective-permute-done((f32[64,8,8]{1,2,0:T(8,128)S(1)}, f32[64,8,8]{1,2,0:T(8,128)S(1)}, u32[]{:S(2)}, u32[]{:S(2)}) %collective-permute-start) | collective-permute-done | bytes 16416 | tf_op jit(solution)/shard_map/ppermute | solution.py:10
  50.1 0.1 copy.10
  50.3 0.1 copy.13
  50.4 3.1 %scatter_fusion.1 = f32[4,16,16,8]{2,3,1,0:T(8,128)S(1)} fusion(f32[4,16,16,8]{2,3,1,0:T(8,128)S(1)} %broadcast_in_dim.45, s32[64]{0:T(128)S(1)} %fusion.11, f32[64,16,8]{1,2,0:T(8,128)S(1)} %copy.13), kind=kCustom, calls=%fused_computation.2 | custom fusion | bytes 98816 | tf_op jit(solution)/shard_map/scatter | solution.py:37
  53.6 0.8 %reshape.118 = f32[4,1,2048]{2,1,0:T(1,128)} reshape(f32[4,16,8,16]{3,2,1,0:T(8,128)S(1)} %bitcast.45) | data formatting | bytes 65536
  54.3 3.3 %all-to-all-start.1 = ((f32[4,1,2048]{2,1,0:T(1,128)}), f32[4,1,2048]{2,1,0:T(1,128)S(1)}, u32[]{:S(2)}, u32[]{:S(2)}) async-start(f32[4,1,2048]{2,1,0:T(1,128)} %reshape.118), calls=%async_computation.1 | async-start | bytes 65536 | tf_op jit(solution)/shard_map/all_to_all | solution.py:70
  57.6 0.1 select_bitcast_fusion
  57.8 0.1 copy.14
  57.9 5.3 %all-to-all-done.1 = f32[4,1,2048]{2,1,0:T(1,128)S(1)} async-done(((f32[4,1,2048]{2,1,0:T(1,128)}), f32[4,1,2048]{2,1,0:T(1,128)S(1)}, u32[]{:S(2)}, u32[]{:S(2)}) %all-to-all-start.1) | async-done | bytes 32800 | tf_op jit(solution)/shard_map/all_to_all | solution.py:70
  63.2 0.5 broadcast.201
  63.7 0.7 reduce.4
  64.5 0.1 reshape.119
  64.6 2.4 %scatter_fusion.2 = f32[64,16,8]{1,2,0:T(8,128)S(1)} fusion(f32[64,16,8]{1,2,0:T(8,128)S(1)} %broadcast.176, s32[64]{0:T(128)S(1)} %fusion.10, f32[64,16,8]{1,2,0:T(8,128)S(1)} %bitcast.46), kind=kCustom, calls=%fused_computation.3 | custom fusion | bytes 98560 | tf_op jit(solution)/shard_map/scatter | solution.py:81
  67.1 0.1 copy.15
  67.2 0.7 copy.16
  (7 shorter events, 0.1 us)
Async XLA Ops:
  7.2 33.1 %all-gather.2.cloned.1.call-start = ((), (), s32[]{:S(2)}) async-start(), calls=%async_computation.2 | async-start | bytes 1310720 | tf_op jit(solution)/shard_map/all_gather | solution.py:64
  20.3 13.0 %all-to-all-start = ((s32[4,1,16]{2,1,0:T(1,128)}), s32[4,1,16]{2,1,0:T(1,128)S(1)}, u32[]{:S(2)}, u32[]{:S(2)}) async-start(s32[4,1,16]{2,1,0:T(1,128)} %bitcast.9), calls=%async_computation | async-start | bytes 4096 | tf_op jit(solution)/shard_map/all_to_all | solution.py:71
  48.5 1.6 %collective-permute-start = (f32[64,8,8]{1,2,0:T(8,128)S(1)}, f32[64,8,8]{1,2,0:T(8,128)S(1)}, u32[]{:S(2)}, u32[]{:S(2)}) collective-permute-start(f32[64,8,8]{1,2,0:T(8,128)S(1)} %get-tuple-element.7), channel_id=1, source_target_pairs={{0,1},{1,0},{2,3},{3,2},{4,5},{5,4},{6,7},{7,6},{8,9},{9,8},{10,11... | collective-permute-start | bytes 49160 | tf_op jit(solution)/shard_map/ppermute | solution.py:10
  54.3 8.9 %all-to-all-start.1 = ((f32[4,1,2048]{2,1,0:T(1,128)}), f32[4,1,2048]{2,1,0:T(1,128)S(1)}, u32[]{:S(2)}, u32[]{:S(2)}) async-start(f32[4,1,2048]{2,1,0:T(1,128)} %reshape.118), calls=%async_computation.1 | async-start | bytes 65536 | tf_op jit(solution)/shard_map/all_to_all | solution.py:70
Sparse Core Ops, SparseCore 0:
  9.6 30.6 all-gather.1
where the time goes:
time: 75.3 us; the launch traced here: 74.7 us
  local copies, waits for them, and re-layouts  22.3 us (30%)
  between operations  14.2 us (19%)
  waiting for transfers between devices  13.1 us (17%)
  starting transfers between devices  9.69 us (13%)
  matrix products  9.14 us (12%)
  other arithmetic  3.94 us (5%)
  blocking collectives  2.39 us (3%)
    scatter x1, local copies, waits for them, and re-layouts, local(): label_buffer = jnp.full((site_count, bucket), -1, jnp.int32).at[target_si...  10.1 us
    all_to_all x1, starting transfers between devices, local(): lax.all_to_all(label_buffer, 'site', split_axis=0, concat_axis=0, tiled=T...  6.32 us
    all_gather x1, waiting for transfers between devices, local(): gathered = lax.all_gather(coeff, 'site', axis=0, tiled=True)  5.71 us
    dot_general x1, matrix products, left_products(): jnp.einsum('euv,ebv->eub', blocks, right_panels, preferred_element_type=j...  5.64 us
    all_to_all x1, waiting for transfers between devices, local(): lax.all_to_all(outgoing, 'site', split_axis=0, concat_axis=0, tiled=True)  5.34 us
    all_to_all x1, starting transfers between devices, local(): lax.all_to_all(outgoing, 'site', split_axis=0, concat_axis=0, tiled=True)  3.26 us
    scatter x1, local copies, waits for them, and re-layouts, left_products(): outgoing = jnp.zeros((site_count, bucket, orb_count, half_orbs), jnp.floa...  3.12 us
    dot_general x1, matrix products, local(): jnp.einsum('kau,kuv->kav', own_panels, fock_site, preferred_element_type=...  2.95 us
  transfers between devices with their start and end apart: 4, of which 3 were waited for; matrix products, arithmetic and copies ran while one was open for 25% of the time, Pallas kernels for 0%

commit v1 on v0

v1 whole, which is shorter than its diff:
```python
import functools

import jax
import jax.numpy as jnp
from jax import lax
from jax.experimental import pallas as pl
from jax.experimental.pallas import tpu as pltpu
from jax.sharding import PartitionSpec as P

F32 = jnp.float32
BF16 = jnp.bfloat16
STEP = 8
ROWS_LAST = (((1,), (1,)), ((), ()))
ROWS_FIRST = (((0,), (0,)), ((), ()))


def iota(shape, axis):
    return lax.broadcasted_iota(jnp.int32, shape, axis)


def as_bf16(flags):
    return jnp.where(flags, 1.0, 0.0).astype(BF16)


def two_parts(value):
    high = value.astype(BF16)
    return high, (value - high.astype(F32)).astype(BF16)


def pick_left(onehot, value):
    high, low = two_parts(value)
    return jnp.dot(onehot, high, preferred_element_type=F32) + jnp.dot(
        onehot, low, preferred_element_type=F32
    )


def pick_right(value, onehot):
    high, low = two_parts(value)
    return jnp.dot(high, onehot, preferred_element_type=F32) + jnp.dot(
        low, onehot, preferred_element_type=F32
    )


def kernel(
    sites, group, half, bucket, own,
    coeff_ref, pair_ref, site_ref, right_ref, out_ref, energy_ref,
    whole, blocks, own_blocks, rights, sent_panels, panels, image_high, image_low,
    pair_rows, payload, arrived,
    load_sem, block_sem, own_sem, orb_sems, right_sems, panel_sems, payload_sems,
):
    site = lax.axis_index("site")
    orb = lax.axis_index("orb")
    pair = lax.axis_index("pair")
    other = 1 - orb
    basis = whole.shape[2]
    panel = bucket * half
    slots = sites * bucket

    load = pltpu.make_async_copy(coeff_ref, whole.at[orb], load_sem)
    load.start()
    own_steps = own // STEP
    steps = group // STEP
    own_loads = []
    for step in range(own_steps):
        part = pl.ds(step * STEP, STEP)
        own_loads.append(pltpu.make_async_copy(site_ref.at[part], own_blocks.at[part], own_sem.at[step]))
        own_loads[-1].start()
    block_loads = []
    for step in range(steps):
        part = pl.ds(step * STEP, STEP)
        block_loads.append(pltpu.make_async_copy(pair_ref.at[part], blocks.at[part], block_sem.at[step]))
        block_loads[-1].start()

    barrier = pltpu.get_barrier_semaphore()
    for ahead in range(sites):
        to_site = lax.rem(site + ahead, sites)
        for cross in range(2):
            if ahead or cross:
                to_orb = other if cross else orb
                pl.semaphore_signal(
                    barrier, inc=1, device_id={"site": to_site, "orb": to_orb},
                    device_id_type=pl.DeviceIdType.MESH,
                )
    pl.semaphore_wait(barrier, 2 * sites - 1)

    right_sends = []
    for ahead in range(1, sites):
        right_sends.append(pltpu.make_async_remote_copy(
            src_ref=right_ref, dst_ref=rights.at[site],
            send_sem=right_sems.at[0, ahead], recv_sem=right_sems.at[1, ahead],
            device_id={"site": lax.rem(site + ahead, sites)},
            device_id_type=pl.DeviceIdType.MESH,
        ))
        right_sends[-1].start()
    orb_send = pltpu.make_async_remote_copy(
        src_ref=coeff_ref, dst_ref=whole.at[orb],
        send_sem=orb_sems.at[0], recv_sem=orb_sems.at[1],
        device_id={"orb": other}, device_id_type=pl.DeviceIdType.MESH,
    )
    orb_send.start()

    rights[site] = right_ref[...]
    upper = as_bf16(iota((group, group), 0) < iota((group, group), 1))
    mine = right_ref[...]
    site_row = iota((sites, group), 0)
    named = (mine >= site_row * group) & (mine < site_row * group + group)
    rank = jnp.dot(as_bf16(named), upper, preferred_element_type=F32).astype(jnp.int32)
    place = jnp.sum(jnp.where(named, site_row * bucket + rank + 1, 0), axis=0, keepdims=True) - 1

    load.wait()
    for send in right_sends:
        send.wait_recv()
    wanted = [None] * sites
    for source in range(sites):
        theirs = rights[source]
        asked = (theirs >= site * group) & (theirs < site * group + group)
        order = jnp.dot(
            as_bf16(jnp.broadcast_to(asked, (8, group))), upper, preferred_element_type=F32
        )[0:1].astype(jnp.int32)
        order = jnp.where(asked, order, -1)
        hit = order == iota((bucket, group), 0)
        local = jnp.sum(jnp.where(hit, theirs - site * group + 1, 0), axis=1, keepdims=True) - 1
        wanted[source] = local
        hit_rows = order == (iota((panel, group), 0) >> 3)
        local_rows = jnp.sum(jnp.where(hit_rows, theirs - site * group + 1, 0), axis=1, keepdims=True) - 1
        row = jnp.where(local_rows >= 0, local_rows * half + (iota((panel, 1), 0) & 7), -1)
        onehot = as_bf16(row == iota((panel, group * half), 1))
        sent_panels[source] = jnp.dot(
            onehot, whole[orb], preferred_element_type=F32
        ).astype(BF16)

    panel_sends = []
    for ahead in range(1, sites):
        to_site = lax.rem(site + ahead, sites)
        panel_sends.append(pltpu.make_async_remote_copy(
            src_ref=sent_panels.at[to_site], dst_ref=panels.at[site],
            send_sem=panel_sems.at[0, ahead], recv_sem=panel_sems.at[1, ahead],
            device_id={"site": to_site}, device_id_type=pl.DeviceIdType.MESH,
        ))
        panel_sends[-1].start()
    panels[site] = sent_panels[site]

    energy = jnp.zeros((half, own), F32)
    lane = iota((half, own), 1)
    for step in range(own_steps):
        own_loads[step].wait()
        for two in range(STEP // 2):
            first = step * STEP + 2 * two
            start = pl.multiple_of((pair * own + first) * half, 2 * half)
            left = whole[orb, pl.ds(start, 2 * half), :]
            wide = left.astype(F32)
            for odd in range(2):
                spread = jnp.dot(left, own_blocks[first + odd], preferred_element_type=F32)
                part = slice(odd * half, (odd + 1) * half)
                total = jnp.sum(spread[part] * wide[part], axis=1, keepdims=True)
                energy = jnp.where(lane == first + odd, total, energy)
    energy_ref[...] = energy

    orb_send.wait_recv()
    for step in range(steps):
        block_loads[step].wait()
        for two in range(STEP // 2):
            first = step * STEP + 2 * two
            rows = pl.ds(first * half, 2 * half)
            left = jnp.concatenate([whole[0, rows, :], whole[1, rows, :]], axis=0)
            one = jnp.dot(left, blocks[first], preferred_element_type=F32)
            nxt = jnp.dot(left, blocks[first + 1], preferred_element_type=F32)
            image = jnp.concatenate(
                [one[:half], nxt[half : 2 * half], one[2 * half : 3 * half], nxt[3 * half :]], axis=0
            )
            high, low = two_parts(image)
            to = pl.ds(first * 2 * half, 4 * half)
            image_high[to, :] = high
            image_low[to, :] = low

    entry_row = iota((group * half, group), 0) >> 3
    place_col = jnp.sum(
        jnp.where(entry_row == iota((group * half, group), 1), place + 1, 0), axis=1, keepdims=True
    ) - 1
    source_row = jnp.where(place_col >= 0, place_col * half + (iota((group * half, 1), 0) & 7), -1)
    reorder = as_bf16(source_row == iota((group * half, slots * half), 1))
    pack = as_bf16(place == iota((slots, group), 0))
    unpack = as_bf16(jnp.concatenate(wanted, axis=0) == iota((slots, group), 1))

    few = basis // half
    rows = few * 2 * half
    row = iota((rows, few * half), 0)
    row_entry = ((row >> 5) << 1) + ((row >> 3) & 1)
    same_entry = row_entry == (iota((rows, few * half), 1) >> 3)
    width = 2 * half * half
    fold = as_bf16((iota((few * half, width), 0) & 7) == ((iota((few * half, width), 1) >> 3) & 7))
    row = iota((rows, width), 0)
    col = iota((rows, width), 1)
    same_orb = (((row >> 4) & 1) == (col >> 6)) & ((row & 7) == (col & 7))
    row = iota((few, rows), 1)
    gather = as_bf16(((row >> 5) << 1) + ((row >> 3) & 1) == iota((few, rows), 0))

    for send in panel_sends:
        send.wait_recv()
    right = jnp.dot(
        reorder, panels[...].reshape(slots * half, basis), preferred_element_type=F32
    ).astype(BF16)
    parts = []
    for index in range(group // few):
        part = right[index * few * half : (index + 1) * few * half]
        span = pl.ds(index * rows, rows)
        full = lax.dot_general(image_high[span, :], part, ROWS_LAST, preferred_element_type=F32)
        full += lax.dot_general(image_low[span, :], part, ROWS_LAST, preferred_element_type=F32)
        folded = pick_right(jnp.where(same_entry, full, 0.0), fold)
        parts.append(pick_left(gather, jnp.where(same_orb, folded, 0.0)))
    by_entry = jnp.concatenate(parts, axis=0)
    payload[...] = pick_left(pack, by_entry).reshape(sites, bucket, width)

    payload_sends = []
    for ahead in range(sites):
        to_site = lax.rem(site + ahead, sites)
        for cross in range(2):
            if ahead or cross:
                payload_sends.append(pltpu.make_async_remote_copy(
                    src_ref=payload.at[to_site], dst_ref=arrived.at[orb, site],
                    send_sem=payload_sems.at[0, 2 * ahead + cross],
                    recv_sem=payload_sems.at[1, 2 * ahead + cross],
                    device_id={"site": to_site, "orb": other if cross else orb},
                    device_id_type=pl.DeviceIdType.MESH,
                ))
                payload_sends[-1].start()
    arrived[orb, site] = payload[site]

    pair_rows[...] = by_entry.T
    for a in range(2 * half):
        start = (a // half) * half * half + a % half
        out_ref[pl.ds(a * 2 * half, half), :] = pair_rows[pl.ds(start, half, stride=half), :]

    for send in payload_sends:
        send.wait_recv()
    for b_half in range(2):
        high, low = two_parts(arrived[b_half].reshape(slots, width))
        moved = lax.dot_general(high, unpack, ROWS_FIRST, preferred_element_type=F32)
        moved += lax.dot_general(low, unpack, ROWS_FIRST, preferred_element_type=F32)
        moved = jnp.where(orb == 0, moved[: half * half], moved[half * half :])
        for b in range(half):
            to = (b_half * half + b) * 2 * half + half
            out_ref[pl.ds(to, half), :] = moved[b * half : (b + 1) * half]

    for send in right_sends + [orb_send] + panel_sends + payload_sends:
        send.wait_send()


def local(sites, coeff, fock_pair, fock_site, pair_right):
    group, half, basis = coeff.shape
    own = fock_site.shape[0]
    bucket = -(-(group // sites) // 8) * 8
    width = 2 * half * half
    dma = pltpu.SemaphoreType.DMA
    any_space = pl.BlockSpec(memory_space=pl.ANY)
    vmem = pl.BlockSpec(memory_space=pltpu.VMEM)
    coupling, energy = pl.pallas_call(
        functools.partial(kernel, sites, group, half, bucket, own),
        out_shape=(
            jax.ShapeDtypeStruct((4 * half * half, group), F32),
            jax.ShapeDtypeStruct((half, own), F32),
        ),
        in_specs=[any_space, any_space, any_space, vmem],
        out_specs=(vmem, vmem),
        scratch_shapes=[
            pltpu.VMEM((2, group * half, basis), BF16),
            pltpu.VMEM((group, basis, basis), BF16),
            pltpu.VMEM((own, basis, basis), BF16),
            pltpu.VMEM((sites, 1, group), jnp.int32),
            pltpu.VMEM((sites, bucket * half, basis), BF16),
            pltpu.VMEM((sites, bucket * half, basis), BF16),
            pltpu.VMEM((group * 2 * half, basis), BF16),
            pltpu.VMEM((group * 2 * half, basis), BF16),
            pltpu.VMEM((width, group), F32),
            pltpu.VMEM((sites, bucket, width), F32),
            pltpu.VMEM((2, sites, bucket, width), F32),
            dma,
            dma((group // STEP,)),
            dma((own // STEP,)),
            dma((2,)),
            dma((2, sites)),
            dma((2, sites)),
            dma((2, 2 * sites)),
        ],
        compiler_params=pltpu.CompilerParams(
            collective_id=0, has_side_effects=True, vmem_limit_bytes=48 * 2**20
        ),
    )(
        coeff.reshape(group * half, basis),
        fock_pair.reshape(group, basis, basis),
        fock_site,
        pair_right.reshape(1, group),
    )
    coupling = coupling.reshape(2 * half, 2, half, group).transpose(3, 0, 1, 2)
    return coupling, energy.T


def solution(mesh):
    return jax.shard_map(
        functools.partial(local, mesh.shape["site"]),
        mesh=mesh,
        in_specs=(
            P(("film", "site"), "orb", None),
            P(("film", "site"), "pair", None, None),
            P(("film", "site", "pair"), None, None),
            P(("film", "site"), "pair"),
        ),
        out_specs=(P(("film", "site"), None, "pair", "orb"), P(("film", "site", "pair"), "orb")),
        check_vma=False,
    )
```

time: 75.3 us -> 28 us (0.37)
  Pallas kernels: 0 us -> 22.1 us
  local copies, waits for them, and re-layouts: 22.3 us -> 5.04 us
  between operations: 14.2 us -> 0.65 us
  waiting for transfers between devices: 13.1 us -> 0 us
  starting transfers between devices: 9.69 us -> 0 us
  matrix products: 9.14 us -> 0 us
  other arithmetic: 3.94 us -> 0 us
  blocking collectives: 2.39 us -> 0 us
    pallas_call x0 -> x1, Pallas kernels: none -> 22.1 us  [local(): pl.pallas_call(functools.partial(kernel, sites, group, half, bucket, own)...]
    scatter x3 -> x0, local copies, waits for them, and re-layouts: 15.7 us -> none  [the longest x1 10.1 us: local(): label_buffer = jnp.full((site_count, bucket), -1, jnp.int32).at[target_si...]
    all_to_all x2 -> x0, starting transfers between devices: 9.58 us -> none  [the longest x1 6.32 us: local(): lax.all_to_all(label_buffer, 'site', split_axis=0, concat_axis=0, tiled=T...]
    dot_general x3 -> x0, matrix products: 9.14 us -> none  [the longest x1 5.64 us: left_products(): jnp.einsum('euv,ebv->eub', blocks, right_panels, preferred_element_type=j...]
    all_gather x1 -> x0, waiting for transfers between devices: 5.71 us -> none  [local(): gathered = lax.all_gather(coeff, 'site', axis=0, tiled=True)]
    all_to_all x2 -> x0, waiting for transfers between devices: 5.35 us -> none  [the longest x1 5.34 us: local(): lax.all_to_all(outgoing, 'site', split_axis=0, concat_axis=0, tiled=True)]
    unnamed x4 -> x8, local copies, waits for them, and re-layouts: 2.23 us -> 5.04 us
    all_gather x1 -> x0, blocking collectives: 2.39 us -> none  [local(): whole_orbs = lax.all_gather(coeff, 'orb', axis=1, tiled=True)]
  transfers between devices with their start and end apart: 4 -> 0, of which waited for: 3 -> 0; matrix products, arithmetic and copies ran while one was open for 25% -> 0% of each run, Pallas kernels for 0% -> 0%
where the time goes in v1:
time: 28 us; the launch traced here: 27.8 us
  Pallas kernels  22.1 us (79%)
  local copies, waits for them, and re-layouts  5.04 us (18%)
  between operations  0.65 us (2%)
    pallas_call x1, Pallas kernels, local(): pl.pallas_call(functools.partial(kernel, sites, group, half, bucket, own)...  22.1 us
    unnamed x8, local copies, waits for them, and re-layouts  5.04 us

profile of v1, /device:TPU:0, one launch (start us, length us, event | category | flops | bytes accessed | tf_op | source)
XLA Modules:
  0.0 27.8 jit_solution(14356087008442389381)
XLA Ops:
  0.6 0.0 copy-start
  0.6 2.2 %copy-done = bf16[32,256,256]{2,1,0:T(8,128)(2,1)S(1)} copy-done((bf16[32,256,256]{2,1,0:T(8,128)(2,1)S(1)}, bf16[32,256,256]{2,1,0:T(8,128)(2,1)}, u32[]{:S(2)}) %copy-start) | copy-done | bytes 4194328
  2.8 0.0 copy-start.1
  2.8 0.9 %copy-done.1 = bf16[64,8,256]{2,1,0:T(8,128)(2,1)S(1)} copy-done((bf16[64,8,256]{2,1,0:T(8,128)(2,1)S(1)}, bf16[64,8,256]{2,1,0:T(8,128)(2,1)}, u32[]{:S(2)}) %copy-start.1) | copy-done | bytes 262168
  3.8 0.0 copy-start.2
  3.8 0.7 %copy-done.2 = s32[64,1]{0,1:T(1,128)S(1)} copy-done((s32[64,1]{0,1:T(1,128)S(1)}, s32[64,1]{0,1:T(1,128)}, u32[]{:S(2)}) %copy-start.2) | copy-done | bytes 280
  4.4 22.1 %shard_map.59 = (f32[256,64]{1,0:T(8,128)S(1)}, f32[8,32]{1,0:T(8,128)S(1)}) custom-call(bf16[512,256]{1,0:T(8,128)(2,1)S(1)} %bitcast.7, bf16[64,256,256]{2,1,0:T(8,128)(2,1)} %bitcast.11, bf16[32,256,256]{2,1,0:T(8,128)(2,1)S(1)} %copy-done, s32[1,64]{1,0:T(1,128)S(1)} %bitcast.10), custom_call_target="tpu_custom_call" | custom-call | tf_op jit(solution)/shard_map/pallas_call | solution.py:257
  26.5 0.7 %copy.8 = f32[64,16,2,8]{0,3,2,1:T(8,128)} copy(f32[64,16,2,8]{0,3,2,1:T(8,128)S(1)} %bitcast.8) | data formatting | bytes 131072
  27.2 0.6 %copy.9 = f32[32,8]{0,1:T(8,128)} copy(f32[32,8]{0,1:T(8,128)S(1)} %bitcast.9) | data formatting | bytes 2048
Async XLA Ops:
  0.6 2.2 %copy-start = (bf16[32,256,256]{2,1,0:T(8,128)(2,1)S(1)}, bf16[32,256,256]{2,1,0:T(8,128)(2,1)}, u32[]{:S(2)}) copy-start(bf16[32,256,256]{2,1,0:T(8,128)(2,1)} %site_ref.1) | copy-start | bytes 12582916
  2.8 0.9 %copy-start.1 = (bf16[64,8,256]{2,1,0:T(8,128)(2,1)S(1)}, bf16[64,8,256]{2,1,0:T(8,128)(2,1)}, u32[]{:S(2)}) copy-start(bf16[64,8,256]{2,1,0:T(8,128)(2,1)} %param.4) | copy-start | bytes 786436
  3.8 0.7 %copy-start.2 = (s32[64,1]{0,1:T(1,128)S(1)}, s32[64,1]{0,1:T(1,128)}, u32[]{:S(2)}) copy-start(s32[64,1]{0,1:T(1,128)} %param.7) | copy-start | bytes 772

commit v2 on v1

v2 whole, which is shorter than its diff:
```python
import functools

import jax
import jax.numpy as jnp
from jax import lax
from jax.experimental import pallas as pl
from jax.experimental.pallas import tpu as pltpu
from jax.sharding import PartitionSpec as P

F32 = jnp.float32
BF16 = jnp.bfloat16
STEP = 8
ROWS_LAST = (((1,), (1,)), ((), ()))
ROWS_FIRST = (((0,), (0,)), ((), ()))


def iota(shape, axis):
    return lax.broadcasted_iota(jnp.int32, shape, axis)


def as_bf16(flags):
    return jnp.where(flags, 1.0, 0.0).astype(BF16)


def two_parts(value):
    high = value.astype(BF16)
    return high, (value - high.astype(F32)).astype(BF16)


def pick_left(onehot, value):
    high, low = two_parts(value)
    return jnp.dot(onehot, high, preferred_element_type=F32) + jnp.dot(
        onehot, low, preferred_element_type=F32
    )


def pick_right(value, onehot):
    high, low = two_parts(value)
    return jnp.dot(high, onehot, preferred_element_type=F32) + jnp.dot(
        low, onehot, preferred_element_type=F32
    )


def peer_of(site, turn):
    peer, bit = site, 1
    while bit <= turn:
        if turn & bit:
            peer = peer + bit - 2 * bit * lax.rem(lax.div(peer, bit), 2)
        bit *= 2
    return peer


def kernel(
    sites, group, half, bucket, own,
    coeff_ref, pair_ref, site_ref, right_ref, out_ref,
    whole, blocks, own_blocks, rights, sent_panels, panels, image, ordered,
    pair_rows, payload, arrived,
    load_sem, mine_sem, block_sem, own_sem, orb_sems, right_sems, panel_sems, payload_sems,
):
    site = lax.axis_index("site")
    orb = lax.axis_index("orb")
    pair = lax.axis_index("pair")
    other = 1 - orb
    basis = whole.shape[2]
    panel = bucket * half
    slots = sites * bucket
    orbs = 2 * half
    rows = bucket * orbs
    peers = [peer_of(site, turn) for turn in range(sites)]

    mine_load = pltpu.make_async_copy(right_ref, rights.at[0], mine_sem)
    mine_load.start()
    load = pltpu.make_async_copy(coeff_ref, whole.at[orb], load_sem)
    load.start()
    barrier = pltpu.get_barrier_semaphore()
    for turn in range(sites):
        for cross in range(2):
            if turn or cross:
                pl.semaphore_signal(
                    barrier, inc=1,
                    device_id={"site": peers[turn], "orb": other if cross else orb},
                    device_id_type=pl.DeviceIdType.MESH,
                )
    own_steps = own // STEP
    steps = group // STEP
    own_loads = []
    for step in range(own_steps):
        part = pl.ds(step * STEP, STEP)
        own_loads.append(pltpu.make_async_copy(site_ref.at[part], own_blocks.at[part], own_sem.at[step]))
        own_loads[-1].start()
    block_loads = []
    for step in range(steps):
        part = pl.ds(step * STEP, STEP)
        block_loads.append(pltpu.make_async_copy(pair_ref.at[part], blocks.at[part], block_sem.at[step]))
        block_loads[-1].start()

    upper = as_bf16(iota((group, group), 0) < iota((group, group), 1))
    mine_load.wait()
    mine = rights[0]
    pl.semaphore_wait(barrier, 2 * sites - 1)

    right_sends = []
    for turn in reversed(range(1, sites)):
        right_sends.append(pltpu.make_async_remote_copy(
            src_ref=rights.at[0], dst_ref=rights.at[turn],
            send_sem=right_sems.at[0, turn], recv_sem=right_sems.at[1, turn],
            device_id={"site": peers[turn]}, device_id_type=pl.DeviceIdType.MESH,
        ))
        right_sends[-1].start()
    orb_send = pltpu.make_async_remote_copy(
        src_ref=coeff_ref, dst_ref=whole.at[orb],
        send_sem=orb_sems.at[0], recv_sem=orb_sems.at[1],
        device_id={"orb": other}, device_id_type=pl.DeviceIdType.MESH,
    )
    orb_send.start()

    peer_row = jnp.zeros((sites, group), jnp.int32)
    for turn in range(sites):
        peer_row = jnp.where(iota((sites, group), 0) == turn, peers[turn], peer_row)
    named = (mine >= peer_row * group) & (mine < peer_row * group + group)
    rank = jnp.dot(as_bf16(named), upper, preferred_element_type=F32).astype(jnp.int32)
    place = jnp.sum(
        jnp.where(named, iota((sites, group), 0) * bucket + rank + 1, 0), axis=0, keepdims=True
    ) - 1

    load.wait()
    for send in right_sends:
        send.wait_recv()
    theirs = jnp.concatenate([rights[turn] for turn in range(sites)], axis=0)
    asked = (theirs >= site * group) & (theirs < site * group + group)
    orders = jnp.dot(as_bf16(asked), upper, preferred_element_type=F32).astype(jnp.int32)
    orders = jnp.where(asked, orders, -1)
    wanted = [None] * sites
    panel_sends = []
    for turn in reversed(range(sites)):
        order = orders[turn : turn + 1]
        found = rights[turn] - site * group + 1
        hit = order == (iota((panel, group), 0) >> 3)
        local_rows = jnp.sum(jnp.where(hit, found, 0), axis=1, keepdims=True) - 1
        row = jnp.where(local_rows >= 0, local_rows * half + (iota((panel, 1), 0) & 7), -1)
        onehot = as_bf16(row == iota((panel, group * half), 1))
        picked = jnp.dot(onehot, whole[orb], preferred_element_type=F32).astype(BF16)
        if turn:
            sent_panels[turn] = picked
            panel_sends.append(pltpu.make_async_remote_copy(
                src_ref=sent_panels.at[turn], dst_ref=panels.at[turn],
                send_sem=panel_sems.at[0, turn], recv_sem=panel_sems.at[1, turn],
                device_id={"site": peers[turn]}, device_id_type=pl.DeviceIdType.MESH,
            ))
            panel_sends[-1].start()
        else:
            panels[0] = picked
    for turn in range(sites):
        hit = orders[turn : turn + 1] == iota((bucket, group), 0)
        found = rights[turn] - site * group + 1
        wanted[turn] = jnp.sum(jnp.where(hit, found, 0), axis=1, keepdims=True) - 1

    orb_send.wait_recv()
    for step in range(steps):
        block_loads[step].wait()
        for two in range(STEP // 2):
            first = step * STEP + 2 * two
            part = pl.ds(first * half, orbs)
            left = jnp.concatenate([whole[0, part, :], whole[1, part, :]], axis=0)
            one = jnp.dot(left, blocks[first], preferred_element_type=F32)
            nxt = jnp.dot(left, blocks[first + 1], preferred_element_type=F32)
            joined = jnp.concatenate(
                [one[:half], nxt[half : 2 * half], one[2 * half : 3 * half], nxt[3 * half :]], axis=0
            )
            high, low = two_parts(joined)
            to = pl.ds(first * orbs, 2 * orbs)
            image[to, :basis] = high
            image[to, basis:] = low

    total_rows = group * orbs
    row = iota((group, total_rows), 1)
    spread_row = as_bf16(((row >> 5) << 1) + ((row >> 3) & 1) == iota((group, total_rows), 0))
    row = iota((1, total_rows), 1)
    key = jnp.dot(
        jnp.broadcast_to(place, (8, group)).astype(F32).astype(BF16), spread_row,
        preferred_element_type=F32,
    )[0:1].astype(jnp.int32)
    key = jnp.where(key >= 0, key * orbs + ((row >> 4) & 1) * half + (row & 7), -1)
    for turn in range(sites):
        onehot = as_bf16(key == iota((rows, total_rows), 0) + turn * rows)
        both = jnp.dot(onehot, image[...], preferred_element_type=F32).astype(BF16)
        ordered[turn, :rows, :] = both[:, :basis]
        ordered[turn, rows:, :] = both[:, basis:]

    energy = jnp.zeros((half, own), F32)
    lane = iota((half, own), 1)
    for step in range(own_steps):
        own_loads[step].wait()
        for two in range(STEP // 2):
            first = step * STEP + 2 * two
            start = pl.multiple_of((pair * own + first) * half, orbs)
            left = whole[orb, pl.ds(start, orbs), :]
            wide = left.astype(F32)
            for odd in range(2):
                spread = jnp.dot(left, own_blocks[first + odd], preferred_element_type=F32)
                part = slice(odd * half, (odd + 1) * half)
                total = jnp.sum(spread[part] * wide[part], axis=1, keepdims=True)
                energy = jnp.where(lane == first + odd, total, energy)
    out_ref[pl.ds(4 * half * half, half), pl.ds(0, own)] = energy

    pack = as_bf16(place == iota((slots, group), 0))
    unpack = as_bf16(jnp.concatenate(wanted, axis=0) == iota((slots, group), 1))
    same_slot = (iota((rows, panel), 0) >> 4) == (iota((rows, panel), 1) >> 3)
    width = 2 * half * half
    fold = as_bf16((iota((panel, width), 0) & 7) == ((iota((panel, width), 1) >> 3) & 7))
    row = iota((rows, width), 0)
    col = iota((rows, width), 1)
    same_orb = ((row >> 3) & 1 == (col >> 6)) & ((row & 7) == (col & 7))

    waits = {turn: send for turn, send in zip(reversed(range(1, sites)), panel_sends)}
    payload_sends = []
    for turn in range(sites):
        if turn:
            waits[turn].wait_recv()
        full = lax.dot_general(ordered[turn], panels[turn], ROWS_LAST, preferred_element_type=F32)
        full = jnp.where(same_slot, full[:rows] + full[rows:], 0.0)
        folded = jnp.where(same_orb, pick_right(full, fold), 0.0)
        payload[turn] = jnp.sum(folded.reshape(bucket, orbs, width), axis=1)
        for cross in range(2):
            if turn or cross:
                payload_sends.append(pltpu.make_async_remote_copy(
                    src_ref=payload.at[turn], dst_ref=arrived.at[orb, turn],
                    send_sem=payload_sems.at[0, 2 * turn + cross],
                    recv_sem=payload_sems.at[1, 2 * turn + cross],
                    device_id={"site": peers[turn], "orb": other if cross else orb},
                    device_id_type=pl.DeviceIdType.MESH,
                ))
                payload_sends[-1].start()
    arrived[orb, 0] = payload[0]

    high, low = two_parts(payload[...].reshape(slots, width))
    by_entry = lax.dot_general(high, pack, ROWS_FIRST, preferred_element_type=F32)
    by_entry += lax.dot_general(low, pack, ROWS_FIRST, preferred_element_type=F32)
    pair_rows[...] = by_entry
    for a in range(orbs):
        start = (a // half) * half * half + a % half
        out_ref[pl.ds(a * orbs, half), :] = pair_rows[pl.ds(start, half, stride=half), :]

    for send in payload_sends:
        send.wait_recv()
    for b_half in range(2):
        high, low = two_parts(arrived[b_half].reshape(slots, width))
        moved = lax.dot_general(high, unpack, ROWS_FIRST, preferred_element_type=F32)
        moved += lax.dot_general(low, unpack, ROWS_FIRST, preferred_element_type=F32)
        moved = jnp.where(orb == 0, moved[: half * half], moved[half * half :])
        for b in range(half):
            to = (b_half * half + b) * orbs + half
            out_ref[pl.ds(to, half), :] = moved[b * half : (b + 1) * half]

    for send in right_sends + [orb_send] + panel_sends + payload_sends:
        send.wait_send()


def local(sites, coeff, fock_pair, fock_site, pair_right):
    group, half, basis = coeff.shape
    own = fock_site.shape[0]
    bucket = -(-(group // sites) // 8) * 8
    width = 2 * half * half
    dma = pltpu.SemaphoreType.DMA
    hbm = pl.BlockSpec(memory_space=pltpu.HBM)
    vmem = pl.BlockSpec(memory_space=pltpu.VMEM)
    joined = pl.pallas_call(
        functools.partial(kernel, sites, group, half, bucket, own),
        out_shape=jax.ShapeDtypeStruct((4 * half * half + half, group), F32),
        in_specs=[hbm] * 4,
        out_specs=vmem,
        scratch_shapes=[
            pltpu.VMEM((2, group * half, basis), BF16),
            pltpu.VMEM((group, basis, basis), BF16),
            pltpu.VMEM((own, basis, basis), BF16),
            pltpu.VMEM((sites, 1, group), jnp.int32),
            pltpu.VMEM((sites, bucket * half, basis), BF16),
            pltpu.VMEM((sites, bucket * half, basis), BF16),
            pltpu.VMEM((group * 2 * half, 2 * basis), BF16),
            pltpu.VMEM((sites, 2 * bucket * 2 * half, basis), BF16),
            pltpu.VMEM((width, group), F32),
            pltpu.VMEM((sites, bucket, width), F32),
            pltpu.VMEM((2, sites, bucket, width), F32),
            dma,
            dma,
            dma((group // STEP,)),
            dma((own // STEP,)),
            dma((2,)),
            dma((2, sites)),
            dma((2, sites)),
            dma((2, 2 * sites)),
        ],
        compiler_params=pltpu.CompilerParams(
            collective_id=0, has_side_effects=True, vmem_limit_bytes=53 * 2**20
        ),
    )(
        coeff.reshape(group * half, basis),
        fock_pair.reshape(group, basis, basis),
        fock_site,
        pair_right.reshape(1, group),
    )
    coupling, energy = joined[: 4 * half * half], joined[4 * half * half :, :own]
    coupling = coupling.reshape(2 * half, 2, half, group).transpose(3, 0, 1, 2)
    return coupling, energy.T


def solution(mesh):
    return jax.shard_map(
        functools.partial(local, mesh.shape["site"]),
        mesh=mesh,
        in_specs=(
            P(("film", "site"), "orb", None),
            P(("film", "site"), "pair", None, None),
            P(("film", "site", "pair"), None, None),
            P(("film", "site"), "pair"),
        ),
        out_specs=(P(("film", "site"), None, "pair", "orb"), P(("film", "site", "pair"), "orb")),
        check_vma=False,
    )
```

time: 28 us -> 24.1 us (0.86)
  local copies, waits for them, and re-layouts: 5.04 us -> 2.86 us
  Pallas kernels: 22.1 us -> 20.5 us
    unnamed x8 -> x4, local copies, waits for them, and re-layouts: 5.04 us -> 1.6 us
    pallas_call x1, Pallas kernels: 22.1 us -> 20.5 us  [local(): pl.pallas_call(functools.partial(kernel, sites, group, half, bucket, own)...]
    slice x0 -> x1, local copies, waits for them, and re-layouts: none -> 0.66 us  [local(): joined[:4 * half * half]]
    transpose x0 -> x1, local copies, waits for them, and re-layouts: none -> 0.6 us  [local(): return (coupling, energy.T)]
where the time goes in v2:
time: 24.1 us; the launch traced here: 24 us
  Pallas kernels  20.5 us (85%)
  local copies, waits for them, and re-layouts  2.86 us (12%)
  between operations  0.65 us (3%)
    pallas_call x1, Pallas kernels, local(): pl.pallas_call(functools.partial(kernel, sites, group, half, bucket, own)...  20.5 us
    unnamed x4, local copies, waits for them, and re-layouts  1.6 us
    slice x1, local copies, waits for them, and re-layouts, local(): joined[:4 * half * half]  0.66 us
    transpose x1, local copies, waits for them, and re-layouts, local(): return (coupling, energy.T)  0.6 us

profile of v2, /device:TPU:0, one launch (start us, length us, event | category | flops | bytes accessed | tf_op | source)
XLA Modules:
  0.0 24.0 jit_solution(9354414278607138245)
XLA Ops:
  0.6 0.0 copy-start
  0.6 0.9 %copy-done = bf16[64,8,256]{2,1,0:T(8,128)(2,1)S(1)} copy-done((bf16[64,8,256]{2,1,0:T(8,128)(2,1)S(1)}, bf16[64,8,256]{2,1,0:T(8,128)(2,1)}, u32[]{:S(2)}) %copy-start) | copy-done | bytes 262168
  1.6 0.0 copy-start.1
  1.6 0.7 %copy-done.1 = s32[64,1]{0,1:T(1,128)S(1)} copy-done((s32[64,1]{0,1:T(1,128)S(1)}, s32[64,1]{0,1:T(1,128)}, u32[]{:S(2)}) %copy-start.1) | copy-done | bytes 280
  2.2 20.5 %shard_map.59 = f32[264,64]{1,0:T(8,128)S(1)} custom-call(bf16[512,256]{1,0:T(8,128)(2,1)S(1)} %bitcast.8, bf16[64,256,256]{2,1,0:T(8,128)(2,1)} %bitcast.10, bf16[32,256,256]{2,1,0:T(8,128)(2,1)} %site_ref.1, s32[1,64]{1,0:T(1,128)S(1)} %bitcast.9), custom_call_target="tpu_custom_call" | custom-call | tf_op jit(solution)/shard_map/pallas_call | solution.py:267
  22.7 0.6 %slice_bitcast_fusion = f32[32,8]{0,1:T(8,128)} fusion(f32[264,64]{1,0:T(8,128)S(1)} %shard_map.59), kind=kLoop, calls=%fused_computation | loop fusion | bytes 2048 | tf_op jit(solution)/shard_map/transpose | solution.py:304
  23.3 0.7 %slice.6 = f32[256,64]{1,0:T(8,128)} slice(f32[264,64]{1,0:T(8,128)S(1)} %shard_map.59), slice={[0:256], [0:64]} | slice | bytes 131072 | tf_op jit(solution)/shard_map/slice | solution.py:302
Async XLA Ops:
  0.6 1.0 %copy-start = (bf16[64,8,256]{2,1,0:T(8,128)(2,1)S(1)}, bf16[64,8,256]{2,1,0:T(8,128)(2,1)}, u32[]{:S(2)}) copy-start(bf16[64,8,256]{2,1,0:T(8,128)(2,1)} %param.4) | copy-start | bytes 786436
  1.6 0.7 %copy-start.1 = (s32[64,1]{0,1:T(1,128)S(1)}, s32[64,1]{0,1:T(1,128)}, u32[]{:S(2)}) copy-start(s32[64,1]{0,1:T(1,128)} %param.7) | copy-start | bytes 772
